TPU v7x, 32 devices: a whole 2x2x4 slice. The times are simulated.
32 devices in a mesh: batch: 16 (over z, y, x), seq: 2 (over core).
Axes of the slice: x: 2, y: 2, z: 4, core: 2. Of those that a mesh axis runs over, the one named last changes fastest.
Arguments:
- inputs: bfloat16 [16, 1024, 768], P('batch', 'seq'), may hold values from -6 to 6
- history: bfloat16 [12, 16, 1024, 768], P(None, 'batch', 'seq'), may hold values from -6 to 6
- segment_ids: int32 [16, 1024], P('batch'), may hold values from 0 to 7, as said below
- cotangent: bfloat16 [16, 1024, 768], P('batch', 'seq'), may hold values from -7 to 7
- mix_weights: float32 [13], replicated, may hold values from 0.2 to 0.8
- attn_gain: bfloat16 [768], P(('batch', 'seq')), may hold values from 0.5 to 1.5
- query_weight: bfloat16 [768, 768], P(('batch', 'seq')), may hold values from -0.21875 to 0.21875
- key_weight: bfloat16 [768, 768], P(('batch', 'seq')), may hold values from -0.21875 to 0.21875
- value_weight: bfloat16 [768, 768], P(('batch', 'seq')), may hold values from -0.21875 to 0.21875
- output_weight: bfloat16 [768, 768], P(('batch', 'seq')), may hold values from -1.5 to 1.5
- mlp_gain: bfloat16 [768], P(('batch', 'seq')), may hold values from 0.5 to 1.5
- up_weight: bfloat16 [768, 3072], P(('batch', 'seq')), may hold values from -0.21875 to 0.21875
- down_weight: bfloat16 [3072, 768], P(('batch', 'seq')), may hold values from -0.109375 to 0.109375
Outputs:
- output: bfloat16 [16, 1024, 768], P('batch', 'seq')
- grad_inputs: float32 [16, 1024, 768], P('batch', 'seq')
- grad_history: bfloat16 [12, 16, 1024, 768], P(None, 'batch', 'seq')
- grad_mix_weights: float32 [13], replicated
- grad_attn_gain: float32 [768], P(('batch', 'seq'))
- grad_query_weight: float32 [768, 768], P(('batch', 'seq'))
- grad_key_weight: float32 [768, 768], P(('batch', 'seq'))
- grad_value_weight: float32 [768, 768], P(('batch', 'seq'))
- grad_output_weight: float32 [768, 768], P(('batch', 'seq'))
- grad_mlp_gain: float32 [768], P(('batch', 'seq'))
- grad_up_weight: float32 [768, 3072], P(('batch', 'seq'))
- grad_down_weight: float32 [3072, 768], P(('batch', 'seq'))
Inputs may be any that keep to these rules, and one draw needn't show every extreme that they name: `segment_ids`: within a row the ids start at 0, never fall, and each id holds one document; in every row one document has tokens on both sides of the row's middle.
All inputs are finite; a program needn't handle non-finite values.
Results may differ from a plain program's by a relative error of at most 0.013.
Values may be sent and summed in bfloat16 or wider, within the bound.
A program may use at most 256 MiB of HBM per device.

v0:
```python
import jax
import jax.numpy as jnp
from jax import lax
from jax.sharding import PartitionSpec as P

HD = 64


EPSILON = 1e-05
MASKED = -1000000000.0


def for_sending(x):
    return jax.tree.map(lambda a: a.astype(jnp.bfloat16) if a.dtype == jnp.float32 else a, x)


def layer_norm(value, gain):
    mean = jnp.mean(value, axis=-1, keepdims=True)
    centred = value - mean
    variance = jnp.mean(centred * centred, axis=-1, keepdims=True)
    return centred * lax.rsqrt(variance + EPSILON) * gain


def rotate(value, angles):
    half = value.shape[-1] // 2
    cosine = jnp.cos(angles)[..., None, :]
    sine = jnp.sin(angles)[..., None, :]
    first = value[..., :half]
    second = value[..., half:]
    return jnp.concatenate(
        [first * cosine - second * sine, second * cosine + first * sine], axis=-1
    )


def frequencies(size):
    return jnp.power(10000.0, -(2.0 / size) * jnp.arange(size // 2, dtype=jnp.float32))


def gelu(value):
    return jax.nn.gelu(value, approximate=True)


def contract_rows(left, right):
    return lax.dot_general(
        left, right, (((0,), (0,)), ((), ())), preferred_element_type=jnp.float32
    )


def contract_cols(left, right):
    return lax.dot_general(
        left, right, (((1,), (1,)), ((), ())), preferred_element_type=jnp.float32
    )


def block_scores(query, keys, segment, first):
    count = query.shape[0]
    length = keys.shape[0]
    scores = jnp.einsum("qhd,khd->hqk", query, keys, preferred_element_type=jnp.float32) * HD ** (
        -0.5
    )
    order_query = first + jnp.arange(count)
    order_key = jnp.arange(length)
    own = segment[first : first + count]
    allowed = (own[:, None] == segment[None, :]) & (order_key[None, :] <= order_query[:, None])
    return jnp.where(allowed[None], scores, MASKED)


def attend_row(packed):
    query, keys, values, segment = packed
    length = query.shape[0]
    heads = query.shape[1] // HD
    query = query.reshape(length, heads, HD)
    keys = keys.reshape(length, heads, HD)
    values = values.reshape(length, heads, HD)
    block = min(512, length)
    mixed_parts = []
    total_parts = []
    for first in range(0, length, block):
        scores = block_scores(query[first : first + block], keys, segment, first)
        top = jnp.max(scores, axis=-1, keepdims=True)
        raw = jnp.exp(scores - top)
        total = jnp.sum(raw, axis=-1, keepdims=True)
        weights = (raw / total).astype(jnp.bfloat16)
        mixed = jnp.einsum("hqk,khd->qhd", weights, values, preferred_element_type=jnp.float32)
        mixed_parts.append(mixed.astype(jnp.bfloat16).reshape(-1, heads * HD))
        total_parts.append((top + jnp.log(total))[..., 0])
    return (jnp.concatenate(mixed_parts, axis=0), jnp.concatenate(total_parts, axis=1))


def attend_back_row(packed):
    query, keys, values, segment, grad_mixed, log_total = packed
    length = query.shape[0]
    heads = query.shape[1] // HD
    query = query.reshape(length, heads, HD)
    keys = keys.reshape(length, heads, HD)
    values = values.reshape(length, heads, HD)
    grad_mixed = grad_mixed.reshape(length, heads, HD)
    scale = HD ** (-0.5)
    block = min(512, length)
    grad_keys = jnp.zeros((length, heads, HD), jnp.float32)
    grad_values = jnp.zeros((length, heads, HD), jnp.float32)
    query_parts = []
    for first in range(0, length, block):
        query_block = query[first : first + block]
        grad_block = grad_mixed[first : first + block]
        scores = block_scores(query_block, keys, segment, first)
        weights = jnp.exp(scores - log_total[:, first : first + block, None])
        grad_weights = jnp.einsum(
            "qhd,khd->hqk", grad_block, values, preferred_element_type=jnp.float32
        )
        inner = jnp.sum(weights * grad_weights, axis=-1, keepdims=True)
        grad_scores = (weights * (grad_weights - inner)).astype(jnp.bfloat16)
        query_parts.append(
            jnp.einsum("hqk,khd->qhd", grad_scores, keys, preferred_element_type=jnp.float32)
            * scale
        )
        grad_keys = (
            grad_keys
            + jnp.einsum(
                "hqk,qhd->khd", grad_scores, query_block, preferred_element_type=jnp.float32
            )
            * scale
        )
        grad_values = grad_values + jnp.einsum(
            "hqk,qhd->khd",
            weights.astype(jnp.bfloat16),
            grad_block,
            preferred_element_type=jnp.float32,
        )
    grad_query = jnp.concatenate(query_parts, axis=0)
    return (
        grad_query.astype(jnp.bfloat16).reshape(length, heads * HD),
        grad_keys.astype(jnp.bfloat16).reshape(length, heads * HD),
        grad_values.astype(jnp.bfloat16).reshape(length, heads * HD),
    )


def local(
    inputs,
    history,
    segment_ids,
    cotangent,
    mix_weights,
    attn_gain,
    query_weight,
    key_weight,
    value_weight,
    output_weight,
    mlp_gain,
    up_weight,
    down_weight,
):
    rows, half_len, width = inputs.shape
    begin = lax.axis_index("seq") * half_len
    tokens = rows * half_len
    heads = width // HD
    gathered = (
        lax.all_gather(attn_gain, ("batch", "seq"), axis=0, tiled=True),
        lax.all_gather(query_weight, ("batch", "seq"), axis=0, tiled=True),
        lax.all_gather(key_weight, ("batch", "seq"), axis=0, tiled=True),
        lax.all_gather(value_weight, ("batch", "seq"), axis=0, tiled=True),
        lax.all_gather(output_weight, ("batch", "seq"), axis=0, tiled=True),
        lax.all_gather(mlp_gain, ("batch", "seq"), axis=0, tiled=True),
        lax.all_gather(up_weight, ("batch", "seq"), axis=0, tiled=True),
        lax.all_gather(down_weight, ("batch", "seq"), axis=0, tiled=True),
    )
    (
        gain_one,
        weight_query,
        weight_key,
        weight_value,
        weight_output,
        gain_two,
        weight_up,
        weight_down,
    ) = gathered
    gain_one = gain_one.astype(jnp.float32)
    gain_two = gain_two.astype(jnp.float32)

    def own_positions(segment_row):
        own = lax.dynamic_slice_in_dim(segment_row, begin, half_len)
        before = jnp.sum((segment_row[None, :] < own[:, None]).astype(jnp.int32), axis=1)
        return begin + jnp.arange(half_len, dtype=jnp.int32) - before

    positions = jax.vmap(own_positions)(segment_ids).reshape(tokens)
    angles = positions[:, None].astype(jnp.float32) * frequencies(HD)
    inputs_flat = inputs.reshape(tokens, width).astype(jnp.float32)
    normed = layer_norm(inputs_flat, gain_one).astype(jnp.bfloat16)
    query_pre = jnp.dot(normed, weight_query, preferred_element_type=jnp.float32).reshape(
        tokens, heads, HD
    )
    key_pre = jnp.dot(normed, weight_key, preferred_element_type=jnp.float32).reshape(
        tokens, heads, HD
    )
    query_turned = rotate(query_pre, angles).astype(jnp.bfloat16).reshape(rows, half_len, width)
    key_turned = rotate(key_pre, angles).astype(jnp.bfloat16).reshape(rows, half_len, width)
    values = (
        jnp.dot(normed, weight_value, preferred_element_type=jnp.float32)
        .astype(jnp.bfloat16)
        .reshape(rows, half_len, width)
    )
    query_heads, key_heads, value_heads = (
        lax.all_to_all(query_turned, "seq", split_axis=2, concat_axis=1, tiled=True),
        lax.all_to_all(key_turned, "seq", split_axis=2, concat_axis=1, tiled=True),
        lax.all_to_all(values, "seq", split_axis=2, concat_axis=1, tiled=True),
    )
    mixed_heads, log_total = lax.map(attend_row, (query_heads, key_heads, value_heads, segment_ids))
    mixed = jax.tree.map(
        lambda part, own: part.astype(own.dtype),
        lax.all_to_all(for_sending(mixed_heads), "seq", split_axis=1, concat_axis=2, tiled=True),
        mixed_heads,
    ).reshape(tokens, width)
    attended = jnp.dot(mixed, weight_output, preferred_element_type=jnp.float32)
    first_sum = inputs_flat + attended
    second_in = layer_norm(first_sum, gain_two).astype(jnp.bfloat16)
    hidden_pre = jnp.dot(second_in, weight_up, preferred_element_type=jnp.float32)
    hidden = gelu(hidden_pre).astype(jnp.bfloat16)
    block_out = first_sum + jnp.dot(hidden, weight_down, preferred_element_type=jnp.float32)
    grad_out = cotangent.reshape(tokens, width).astype(jnp.float32)
    output = mix_weights[-1] * block_out
    mix_terms = []
    for index in range(history.shape[0]):
        earlier = history[index].reshape(tokens, width).astype(jnp.float32)
        output = output + mix_weights[index] * earlier
        mix_terms.append(jnp.sum(earlier * grad_out))
    mix_terms.append(jnp.sum(block_out * grad_out))
    grad_mix = lax.psum(jnp.stack(mix_terms), ("batch", "seq"))
    grad_history = (
        mix_weights[:-1, None, None, None] * cotangent.astype(jnp.float32)[None]
    ).astype(jnp.bfloat16)
    gathered = (
        lax.all_gather(attn_gain, ("batch", "seq"), axis=0, tiled=True),
        lax.all_gather(query_weight, ("batch", "seq"), axis=0, tiled=True),
        lax.all_gather(key_weight, ("batch", "seq"), axis=0, tiled=True),
        lax.all_gather(value_weight, ("batch", "seq"), axis=0, tiled=True),
        lax.all_gather(output_weight, ("batch", "seq"), axis=0, tiled=True),
        lax.all_gather(mlp_gain, ("batch", "seq"), axis=0, tiled=True),
        lax.all_gather(up_weight, ("batch", "seq"), axis=0, tiled=True),
        lax.all_gather(down_weight, ("batch", "seq"), axis=0, tiled=True),
    )
    (
        gain_one,
        weight_query,
        weight_key,
        weight_value,
        weight_output,
        gain_two,
        weight_up,
        weight_down,
    ) = gathered
    gain_one = gain_one.astype(jnp.float32)
    gain_two = gain_two.astype(jnp.float32)
    grad_block = mix_weights[-1] * grad_out
    grad_block_low = grad_block.astype(jnp.bfloat16)
    grad_down = contract_rows(hidden, grad_block_low)
    grad_hidden = contract_cols(grad_block_low, weight_down)
    grad_hidden_pre = jax.vjp(gelu, hidden_pre)[1](grad_hidden)[0].astype(jnp.bfloat16)
    grad_up = contract_rows(second_in, grad_hidden_pre)
    grad_second = contract_cols(grad_hidden_pre, weight_up)
    grad_first_part, grad_gain_two = jax.vjp(layer_norm, first_sum, gain_two)[1](grad_second)
    grad_first = grad_block + grad_first_part
    grad_first_low = grad_first.astype(jnp.bfloat16)
    grad_output = contract_rows(mixed, grad_first_low)
    grad_mixed = (
        contract_cols(grad_first_low, weight_output)
        .astype(jnp.bfloat16)
        .reshape(rows, half_len, width)
    )
    grad_mixed_heads = lax.all_to_all(grad_mixed, "seq", split_axis=2, concat_axis=1, tiled=True)
    grad_query_heads, grad_key_heads, grad_value_heads = lax.map(
        attend_back_row,
        (query_heads, key_heads, value_heads, segment_ids, grad_mixed_heads, log_total),
    )
    grad_query_turned, grad_key_turned, grad_values = (
        lax.all_to_all(grad_query_heads, "seq", split_axis=1, concat_axis=2, tiled=True),
        lax.all_to_all(grad_key_heads, "seq", split_axis=1, concat_axis=2, tiled=True),
        lax.all_to_all(grad_value_heads, "seq", split_axis=1, concat_axis=2, tiled=True),
    )

    def turn(value):
        return rotate(value, angles)

    turn_back = jax.vjp(turn, query_pre)[1]
    grad_query_pre = (
        turn_back(grad_query_turned.reshape(tokens, heads, HD).astype(jnp.float32))[0]
        .reshape(tokens, width)
        .astype(jnp.bfloat16)
    )
    grad_key_pre = (
        turn_back(grad_key_turned.reshape(tokens, heads, HD).astype(jnp.float32))[0]
        .reshape(tokens, width)
        .astype(jnp.bfloat16)
    )
    grad_values = grad_values.reshape(tokens, width)
    grad_query_w = contract_rows(normed, grad_query_pre)
    grad_key_w = contract_rows(normed, grad_key_pre)
    grad_value_w = contract_rows(normed, grad_values)
    grad_normed = (
        contract_cols(grad_query_pre, weight_query)
        + contract_cols(grad_key_pre, weight_key)
        + contract_cols(grad_values, weight_value)
    )
    grad_in_part, grad_gain_one = jax.vjp(layer_norm, inputs_flat, gain_one)[1](grad_normed)
    grad_inputs = (grad_first + grad_in_part).reshape(rows, half_len, width)
    shares = (
        lax.psum_scatter(grad_gain_one, ("batch", "seq"), scatter_dimension=0, tiled=True),
        lax.psum_scatter(grad_query_w, ("batch", "seq"), scatter_dimension=0, tiled=True),
        lax.psum_scatter(grad_key_w, ("batch", "seq"), scatter_dimension=0, tiled=True),
        lax.psum_scatter(grad_value_w, ("batch", "seq"), scatter_dimension=0, tiled=True),
        lax.psum_scatter(grad_output, ("batch", "seq"), scatter_dimension=0, tiled=True),
        lax.psum_scatter(grad_gain_two, ("batch", "seq"), scatter_dimension=0, tiled=True),
        lax.psum_scatter(grad_up, ("batch", "seq"), scatter_dimension=0, tiled=True),
        lax.psum_scatter(grad_down, ("batch", "seq"), scatter_dimension=0, tiled=True),
    )
    return (
        output.astype(jnp.bfloat16).reshape(rows, half_len, width),
        grad_inputs,
        grad_history,
        grad_mix,
        shares[0],
        shares[1],
        shares[2],
        shares[3],
        shares[4],
        shares[5],
        shares[6],
        shares[7],
    )


def solution(mesh):
    placed = (
        P("batch", "seq", None),
        P(None, "batch", "seq", None),
        P("batch", None),
        P("batch", "seq", None),
        P(),
        P(("batch", "seq")),
        P(("batch", "seq"), None),
        P(("batch", "seq"), None),
        P(("batch", "seq"), None),
        P(("batch", "seq"), None),
        P(("batch", "seq")),
        P(("batch", "seq"), None),
        P(("batch", "seq"), None),
    )
    return jax.shard_map(
        local,
        mesh=mesh,
        in_specs=placed,
        out_specs=(
            P("batch", "seq", None),
            P("batch", "seq", None),
            P(None, "batch", "seq", None),
            P(),
            P(("batch", "seq")),
            P(("batch", "seq"), None),
            P(("batch", "seq"), None),
            P(("batch", "seq"), None),
            P(("batch", "seq"), None),
            P(("batch", "seq")),
            P(("batch", "seq"), None),
            P(("batch", "seq"), None),
        ),
        check_vma=False,
    )
```

profile of v0, /device:TPU:0, one launch (start us, length us, event | category | flops | bytes accessed | tf_op | source)
XLA Modules:
  0.0 1125.7 jit_solution(11040111078522410057)
XLA Ops:
  13.5 42.0 %all-reduce.9 = (bf16[768]{0:T(1024)(128)(2,1)S(1)}, bf16[768]{0:T(1024)(128)(2,1)S(1)}) all-reduce(bf16[768]{0:T(1024)(128)(2,1)S(1)} %dynamic-update-slice.1, bf16[768]{0:T(1024)(128)(2,1)S(1)} %dynamic-update-slice.2), channel_id=1, replica_groups=mesh['batch'=16,'seq'=2] {'batch','seq'}, use_global_device_ids=true, to_apply=%add.4 | all-reduce | flops 1536 | bytes 6144
  59.0 8.8 all-gather.7.cloned.1.call-done
  67.8 3.0 fusion.66
  70.8 3.5 copy.99
  74.8 6.3 reduce.2
  82.8 5.3 all_to_all.108
  91.4 32.3 %all-gather.11.cloned.1.call-done = bf16[768,768]{1,0:T(8,128)(2,1)} async-done(((bf16[24,768]{1,0:T(8,128)(2,1)}), bf16[768,768]{1,0:T(8,128)(2,1)}) %all-gather.11.cloned.1.call-update) | async-done | bytes 1179664 | tf_op jit(solution)/shard_map/all_gather | solution.py:160
  126.1 3.4 fusion.74
  129.4 50.2 %all-gather.9.cloned.1.call-done = bf16[768,768]{1,0:T(8,128)(2,1)} async-done(((bf16[24,768]{1,0:T(8,128)(2,1)}), bf16[768,768]{1,0:T(8,128)(2,1)}) %all-gather.9.cloned.1.call-update) | async-done | bytes 1179664 | tf_op jit(solution)/shard_map/all_gather | solution.py:159
  188.3 6.4 reduce.4
  196.1 5.8 all_to_all.109
  209.3 3.5 copy.131
  212.8 7.3 reduce.3
  222.4 6.6 all_to_all.110
  235.7 2.8 fusion.1
  240.3 3.9 fusion.70
  246.2 3.4 fusion.110
  249.6 2.8 fusion
  254.1 4.1 fusion.71
  263.6 7.3 reduce.5
  272.8 6.8 all_to_all.111
  290.8 10.0 all-gather.15.cloned.1.call-done
  300.8 8.2 fusion.98
  309.0 57.0 %all-gather.17.cloned.1.call-done = bf16[3072,768]{1,0:T(8,128)(2,1)} async-done(((bf16[96,768]{1,0:T(8,128)(2,1)}), bf16[3072,768]{1,0:T(8,128)(2,1)}) %all-gather.17.cloned.1.call-update) | async-done | bytes 4718608 | tf_op jit(solution)/shard_map/all_gather | solution.py:165
  366.0 9.7 fusion.10
  375.8 2.9 multiply_reduce_fusion.2
  382.0 10.1 fusion.61
  395.2 3.2 fusion.67
  398.4 4.8 copy.110
  403.1 7.3 reduce.6
  412.7 6.3 all_to_all.112
  419.1 2.6 reshape.688
  424.2 5.9 fusion.11
  430.1 7.0 add_convert_fusion
  437.1 4.8 copy.118
  442.0 7.3 reduce.7
  451.2 6.6 all_to_all.113
  457.8 2.6 reshape.694
  465.2 3.5 fusion.80
  468.7 9.7 multiply_reduce_fusion.1
  478.3 8.9 multiply_reduce_fusion
  487.4 9.7 multiply_convert_fusion.2
  498.4 3.3 slice-done.2
  501.7 9.1 multiply_convert_fusion.1
  514.6 4.8 fusion.69
  521.6 3.4 fusion.112
  525.0 6.3 reduce.9
  532.6 5.3 all_to_all.114
  541.0 3.2 copy.114
  544.2 4.3 fusion.114
  550.7 4.2 copy.115
  554.9 6.3 reduce.8
  562.4 5.1 all_to_all.115
  581.8 10.4 fusion.88
  593.7 7.2 fusion.97
  602.1 6.1 multiply_convert_fusion
  608.2 8.2 stack.55
  622.0 40.1 %all-reduce.8 = (f32[13]{0:T(128)}, f32[768]{0:T(1024)S(1)}, f32[768]{0:T(1024)S(1)}) all-reduce(f32[13]{0:T(128)S(1)} %stack.55, f32[768]{0:T(1024)S(1)} %get-tuple-element.88, f32[768]{0:T(1024)S(1)} %get-tuple-element.86), channel_id=1, replica_groups=mesh['batch'=16,'seq'=2] {'batch','seq'}, use_global_device_ids=true, to_apply=%region_28.29 | all-reduce | flops 1549 | bytes 12392 | tf_op jit(solution)/shard_map/psum | solution.py:227
  663.3 4.2 add_bitcast_fusion
  667.4 13.4 %fusion.87 = bf16[1,512,768]{2,1,0:T(8,128)(2,1)} fusion(f32[]{:T(128)} %bitcast.49, f32[]{:T(128)} %bitcast.47, f32[]{:T(128)} %bitcast.45, f32[]{:T(128)} %bitcast.43, f32[]{:T(128)} %bitcast.41, f32[]{:T(128)} %bitcast.39, f32[]{:T(128)} %bitcast.37, f32[]{:T(128)} %bitcast.35, f32[]{:T(128)} %bitcast.33, f32[]{:T(128)} %bitcast.31, f32[]{:T(128)} %bitcast.29, ...), kind=kLoop, calls=%fused_computation.162 | loop fusion | flops 14942208 | bytes 11796532 | tf_op jit(solution)/shard_map/reshape | solution.py:316
  680.9 50.0 %reduce-scatter.7.cloned.1.call-done = f32[24,768]{1,0:T(8,128)} async-done(((f32[768,768]{1,0:T(8,128)}), f32[24,768]{1,0:T(8,128)}) %reduce-scatter.7.cloned.1.call-update) | async-done | bytes 73744 | tf_op jit(solution)/shard_map/reduce_scatter | solution.py:307
  730.9 104.7 %reduce-scatter.9.cloned.1.call-done = f32[24,768]{1,0:T(8,128)} async-done(((f32[768,768]{1,0:T(8,128)}), f32[24,768]{1,0:T(8,128)}) %reduce-scatter.9.cloned.1.call-update) | async-done | bytes 73744 | tf_op jit(solution)/shard_map/reduce_scatter | solution.py:308
  835.5 141.2 %reduce-scatter.17.cloned.1.call-done = f32[96,768]{1,0:T(8,128)} async-done(((f32[3072,768]{1,0:T(8,128)}), f32[96,768]{1,0:T(8,128)}) %reduce-scatter.17.cloned.1.call-update) | async-done | bytes 294928 | tf_op jit(solution)/shard_map/reduce_scatter | solution.py:313
  976.7 141.9 %reduce-scatter.15.cloned.1.call-done = f32[24,3072]{1,0:T(8,128)} async-done(((f32[768,3072]{1,0:T(8,128)}), f32[24,3072]{1,0:T(8,128)}) %reduce-scatter.15.cloned.1.call-update) | async-done | bytes 294928 | tf_op jit(solution)/shard_map/reduce_scatter | solution.py:312
  (211 shorter events, 124.0 us)
Async XLA Ops:
  7.2 5.4 copy-start.3
  7.2 5.8 copy-start.38
  7.2 6.1 copy-start.39
  7.2 48.3 %copy-start.33 = (s32[1,1024]{1,0:T(1,128)S(1)}, s32[1,1024]{1,0:T(1,128)}, u32[]{:S(2)}) copy-start(s32[1,1024]{1,0:T(1,128)} %param.15) | copy-start | bytes 12292
  7.2 48.7 %copy-start.31 = (f32[13]{0:T(128)S(1)}, f32[13]{0:T(128)}, u32[]{:S(2)}) copy-start(f32[13]{0:T(128)} %param.17) | copy-start | bytes 160
  7.2 60.6 %all-gather.7.cloned.1.call-start = ((), (), s32[]{:S(2)}) async-start(), calls=%async_computation.14 | async-start | bytes 1216512 | tf_op jit(solution)/shard_map/all_gather | solution.py:161
  8.0 115.7 %all-gather.11.cloned.1.call-start = ((), (), s32[]{:S(2)}) async-start(), calls=%async_computation.16 | async-start | bytes 1216512 | tf_op jit(solution)/shard_map/all_gather | solution.py:160
  8.7 170.9 %all-gather.9.cloned.1.call-start = ((), (), s32[]{:S(2)}) async-start(), calls=%async_computation.15 | async-start | bytes 1216512 | tf_op jit(solution)/shard_map/all_gather | solution.py:159
  9.4 277.4 %all-gather.13.cloned.1.call-start = ((), (), s32[]{:S(2)}) async-start(), calls=%async_computation.17 | async-start | bytes 1216512 | tf_op jit(solution)/shard_map/all_gather | solution.py:162
  10.0 290.8 %all-gather.15.cloned.1.call-start = ((), (), s32[]{:S(2)}) async-start(), calls=%async_computation.18 | async-start | bytes 4866048 | tf_op jit(solution)/shard_map/all_gather | solution.py:164
  10.6 355.4 %all-gather.17.cloned.1.call-start = ((), (), s32[]{:S(2)}) async-start(), calls=%async_computation.19 | async-start | bytes 4866048 | tf_op jit(solution)/shard_map/all_gather | solution.py:165
  11.2 669.7 %reduce-scatter.13.cloned.1.call-start = ((), (), s32[]{:S(2)}) async-start(), calls=%async_computation.23 | async-start | bytes 2433024 | tf_op jit(solution)/shard_map/reduce_scatter | solution.py:310
  13.0 42.6 %copy-start.34 = (f32[512]{0:T(512)}, f32[512]{0:T(512)S(1)}, u32[]{:S(2)}) copy-start(f32[512]{0:T(512)S(1)} %fusion.45) | copy-start | bytes 6148
  57.0 127.3 %copy-start.27 = (f32[512,32]{0,1:T(8,128)}, f32[512,32]{0,1:T(8,128)S(1)}, u32[]{:S(2)}) copy-start(f32[512,32]{0,1:T(8,128)S(1)} %get-tuple-element.120) | copy-start | bytes 196612
  57.0 127.3 %copy-start.29 = (f32[512,32]{0,1:T(8,128)}, f32[512,32]{0,1:T(8,128)S(1)}, u32[]{:S(2)}) copy-start(f32[512,32]{0,1:T(8,128)S(1)} %get-tuple-element.121) | copy-start | bytes 196612
  182.0 2.4 copy-start.19
  231.5 1.8 copy-start.16
  233.3 12.9 %copy-start.8 = (bf16[1,1,512,384]{2,3,1,0:T(8,128)(2,1)}, bf16[1,1,512,384]{2,3,1,0:T(8,128)(2,1)S(1)}, u32[]{:S(2)}) copy-start(bf16[1,1,512,384]{2,3,1,0:T(8,128)(2,1)S(1)} %get-tuple-element.109) | copy-start | bytes 1179652
  235.7 4.6 copy-start.1
  249.6 4.5 copy-start
  254.1 6.1 copy-start.18
  289.3 1.1 copy-start.4
  366.0 9.7 copy-start.5
  366.0 9.7 copy-start.37
  375.7 2.9 copy-start.15
  375.8 3.6 copy-start.36
  375.8 5.9 copy-start.40
  378.7 3.3 copy-start.12
  379.3 12.8 %copy-start.7 = (f32[512,768]{1,0:T(8,128)}, f32[512,768]{1,0:T(8,128)S(1)}, u32[]{:S(2)}) copy-start(f32[512,768]{1,0:T(8,128)S(1)} %get-tuple-element.97) | copy-start | bytes 4718596
  382.0 10.9 copy-start.11
  392.1 0.9 copy-start.26
  424.2 256.7 %reduce-scatter.11.cloned.1.call-start = ((), (), s32[]{:S(2)}) async-start(), calls=%async_computation.22 | async-start | bytes 2433024 | tf_op jit(solution)/shard_map/reduce_scatter | solution.py:309
  424.2 5.9 copy-start.9
  487.3 243.6 %reduce-scatter.7.cloned.1.call-start = ((), (), s32[]{:S(2)}) async-start(), calls=%async_computation.20 | async-start | bytes 2433024 | tf_op jit(solution)/shard_map/reduce_scatter | solution.py:307
  487.3 9.8 slice-start
  487.3 11.1 slice-start.1
  487.4 14.4 %slice-start.2 = ((s8[12582912]{0:T(1024)(128)(4,1)}), s8[4194304]{0:T(1024)(128)(4,1)S(1)}, s32[]{:S(2)}) async-start(s8[12582912]{0:T(1024)(128)(4,1)} %bitcast.312), calls=%async_computation.28 | async-start | bytes 8388608
  497.1 13.7 %copy-start.2 = (bf16[6,512,1024]{2,1,0:T(8,128)(2,1)}, bf16[6,512,1024]{2,1,0:T(8,128)(2,1)S(1)}, u32[]{:S(2)}) copy-start(bf16[6,512,1024]{2,1,0:T(8,128)(2,1)S(1)} %multiply_convert_fusion.2) | copy-start | bytes 18874372
  541.0 7.6 slice-start.3
  544.2 4.4 slice-start.4
  569.5 1.6 copy-start.28
  569.5 1.6 copy-start.30
  573.6 0.9 copy-start.23
  576.9 258.6 %reduce-scatter.9.cloned.1.call-start = ((), (), s32[]{:S(2)}) async-start(), calls=%async_computation.21 | async-start | bytes 2433024 | tf_op jit(solution)/shard_map/reduce_scatter | solution.py:308
  577.3 0.9 copy-start.25
  580.7 1.1 copy-start.13
  580.7 396.0 %reduce-scatter.17.cloned.1.call-start = ((), (), s32[]{:S(2)}) async-start(), calls=%async_computation.25 | async-start | bytes 9732096 | tf_op jit(solution)/shard_map/reduce_scatter | solution.py:313
  592.3 1.4 copy-start.6
  592.3 526.3 %reduce-scatter.15.cloned.1.call-start = ((), (), s32[]{:S(2)}) async-start(), calls=%async_computation.24 | async-start | bytes 9732096 | tf_op jit(solution)/shard_map/reduce_scatter | solution.py:312
  600.8 1.1 copy-start.14
  600.9 1.2 copy-start.32
  602.1 14.3 %copy-start.20 = (bf16[768,768]{1,0:T(8,128)(2,1)S(1)}, bf16[768,768]{1,0:T(8,128)(2,1)}, u32[]{:S(2)}) copy-start(bf16[768,768]{1,0:T(8,128)(2,1)} %all-gather.11.cloned.1.call-done) | copy-start | bytes 3538948
  616.4 2.1 copy-start.21
  616.4 2.1 copy-start.24
  618.5 1.1 copy-start.10
  618.5 1.5 copy-start.22
  620.1 1.2 copy-start.35
  663.3 4.2 copy-start.17
Sparse Core Ops, SparseCore 0:
  11.0 56.7 all-gather.6
  70.7 52.9 all-gather.10
  126.6 52.9 all-gather.8
  182.4 52.9 all-gather.12
  238.1 62.6 all-gather.14
  303.6 62.4 all-gather.16
  424.3 97.7 reduce-scatter.12
  528.8 98.1 reduce-scatter.10
  632.8 97.9 reduce-scatter.6
  737.4 98.0 reduce-scatter.8
  842.0 134.6 reduce-scatter.16
  984.0 134.4 reduce-scatter.14
where the time goes:
time: 1140 us; the launch traced here: 1130 us
  waiting for transfers between devices  600 us (53%)
  matrix products  136 us (12%)
  blocking collectives  130 us (11%)
  local copies, waits for them, and re-layouts  125 us (11%)
  other arithmetic  119 us (10%)
  between operations  15.3 us (1%)
    reduce_scatter x1, waiting for transfers between devices, local(): lax.psum_scatter(grad_up, ('batch', 'seq'), scatter_dimension=0, tiled=True)  142 us
    reduce_scatter x1, waiting for transfers between devices, local(): lax.psum_scatter(grad_down, ('batch', 'seq'), scatter_dimension=0, tiled=...  141 us
    reduce_scatter x1, waiting for transfers between devices, local(): lax.psum_scatter(grad_key_w, ('batch', 'seq'), scatter_dimension=0, tiled...  105 us
    unnamed x121, local copies, waits for them, and re-layouts  61.9 us
    unnamed x11, other arithmetic  57.9 us
    all_gather x1, waiting for transfers between devices, local(): lax.all_gather(down_weight, ('batch', 'seq'), axis=0, tiled=True)  57 us
    all_gather x1, waiting for transfers between devices, local(): lax.all_gather(query_weight, ('batch', 'seq'), axis=0, tiled=True)  50.2 us
    reduce_scatter x1, waiting for transfers between devices, local(): lax.psum_scatter(grad_query_w, ('batch', 'seq'), scatter_dimension=0, til...  50 us
  transfers between devices with their start and end apart: 12, of which 9 were waited for; matrix products, arithmetic and copies ran while one was open for 28% of the time, Pallas kernels for 0%

commit v1 on v0

v1 whole, which is shorter than its diff:
```python
import functools

import jax
import jax.numpy as jnp
import numpy as np
from jax import lax
from jax.experimental import pallas as pl
from jax.experimental.pallas import tpu as pltpu
from jax.sharding import PartitionSpec as P

HD = 64
EPSILON = 1e-05
MASKED = -1000000000.0
MESH = pl.DeviceIdType.MESH
F32 = jnp.float32
BF16 = jnp.bfloat16
NZ, NY, NX = 4, 2, 2
GROUPS = NZ * NY * NX
COPIES = 224
BLOCK = 256


def mm(a, b):
    return lax.dot_general(a, b, (((1,), (0,)), ((), ())), preferred_element_type=F32)


def mm_nt(a, b):
    return lax.dot_general(a, b, (((1,), (1,)), ((), ())), preferred_element_type=F32)


def mm_tn(a, b):
    return lax.dot_general(a, b, (((0,), (0,)), ((), ())), preferred_element_type=F32)


def loop(count, body):
    def step(i, carry):
        body(i)
        return carry

    lax.fori_loop(0, count, step, 0)


def rows_of(i, size):
    return pl.ds(pl.multiple_of(i * size, size), size)


def lane_cut(start, size):
    return pl.ds(pl.multiple_of(start, 128), size)


def normalize(value):
    mean = jnp.mean(value, axis=-1, keepdims=True)
    centred = value - mean
    variance = jnp.mean(centred * centred, axis=-1, keepdims=True)
    root = lax.rsqrt(variance + EPSILON)
    return centred * root, root


def norm_back(xhat, root, gain, grad):
    g = grad * gain
    return root * (
        g - jnp.mean(g, axis=-1, keepdims=True) - xhat * jnp.mean(g * xhat, axis=-1, keepdims=True)
    )


def fold_rows(value):
    total = value[0:8]
    for r in range(8, value.shape[0], 8):
        total = total + value[r : r + 8]
    return total


class Place:
    def __init__(self, unit):
        batch = lax.axis_index("batch")
        self.k = lax.axis_index("seq")
        self.o = 1 - self.k
        group = batch // unit
        self.unit = unit
        self.u = batch % unit
        self.z = group // (NY * NX)
        self.y = (group // NX) % NY
        self.x = group % NX
        self.core = (batch, self.o)
        self.xn = self.device(self.z, self.y, 1 - self.x)
        self.yn = self.device(self.z, 1 - self.y, self.x)

    def device(self, z, y, x):
        return (((z * NY + y) * NX + x) * self.unit + self.u, self.k)

    def ahead(self, step):
        return (self.z + step) % NZ

    def behind(self, step):
        return (self.z + NZ - step) % NZ

    def zn(self, step):
        return self.device(self.ahead(step), self.y, self.x)


class Wire:
    def __init__(self, send, recv):
        self.send = send
        self.recv = recv
        self.open = []
        self.count = 0

    def copy(self, src, dst, device):
        i = self.count
        self.count += 1
        made = pltpu.make_async_remote_copy(
            src_ref=src,
            dst_ref=dst,
            send_sem=self.send.at[i],
            recv_sem=self.recv.at[i],
            device_id=device,
            device_id_type=MESH,
        )
        made.start()
        self.open.append(made)
        return made

    def sent(self, made):
        made.wait_send()
        self.open = [one for one in self.open if one is not made]

    def close(self):
        for made in self.open:
            made.wait_send()


class Gather:
    def __init__(self, wire, at, ref, cut):
        self.wire, self.at, self.ref, self.cut = wire, at, ref, cut
        self.z = {}
        self.mid = {}
        self.last = {}

    def start(self):
        at, ref = self.at, self.ref
        own = ref.at[at.z, at.y, at.x]
        for step in range(1, NZ):
            self.z[step] = self.wire.copy(own, own, at.zn(step))
        self.pass_mid(0)

    def pass_mid(self, step):
        at, ref, cut = self.at, self.ref, self.cut
        if step:
            self.z[step].wait_recv()
        zz = at.behind(step)
        left = ref.at[zz, at.y, at.x, :, :cut]
        right = ref.at[zz, at.y, at.x, :, cut:]
        self.mid[step] = (
            self.wire.copy(left, left, at.xn),
            self.wire.copy(right, right, at.yn),
        )

    def pass_last(self, step):
        at, ref, cut = self.at, self.ref, self.cut
        zz = at.behind(step)
        self.mid[step][0].wait_recv()
        left = ref.at[zz, at.y, :, :, :cut]
        one = self.wire.copy(left, left, at.yn)
        self.mid[step][1].wait_recv()
        right = ref.at[zz, :, at.x, :, cut:]
        self.last[step] = (one, self.wire.copy(right, right, at.xn))

    def finish(self):
        for step in range(NZ):
            for made in self.last[step]:
                made.wait_recv()

    def steps(self):
        return [
            self.start,
            lambda: (self.pass_mid(1), self.pass_last(0)),
            lambda: (self.pass_mid(2), self.pass_last(1)),
            lambda: (self.pass_mid(3), self.pass_last(2)),
            lambda: self.pass_last(3),
        ]


class Reduce:
    def __init__(self, wire, at, grad, cut, one_a, one_b, two, three):
        self.wire, self.at, self.grad, self.cut = wire, at, grad, cut
        self.one_a, self.one_b, self.two, self.three = one_a, one_b, two, three

    def first(self):
        at, grad, cut = self.at, self.grad, self.cut
        self.a = self.wire.copy(grad.at[:, 1 - at.y, :, :, :cut], self.one_a, at.yn)
        self.b = self.wire.copy(grad.at[:, :, 1 - at.x, :, cut:], self.one_b, at.xn)

    def second(self):
        at, grad, cut = self.at, self.grad, self.cut
        self.a.wait_recv()

        def add_a(xx):
            def body(zz):
                grad[zz, at.y, xx, :, :cut] = (
                    grad[zz, at.y, xx, :, :cut].astype(F32) + self.one_a[zz, xx].astype(F32)
                ).astype(BF16)

            loop(NZ, body)

        def add_b(yy):
            def body(zz):
                grad[zz, yy, at.x, :, cut:] = (
                    grad[zz, yy, at.x, :, cut:].astype(F32) + self.one_b[zz, yy].astype(F32)
                ).astype(BF16)

            loop(NZ, body)

        add_a(1 - at.x)
        self.aa = self.wire.copy(
            grad.at[:, at.y, 1 - at.x, :, :cut], self.two.at[:, :, :cut], at.xn
        )
        self.b.wait_recv()
        add_b(1 - at.y)
        self.bb = self.wire.copy(
            grad.at[:, 1 - at.y, at.x, :, cut:], self.two.at[:, :, cut:], at.yn
        )
        add_a(at.x)
        add_b(at.y)

    def third(self):
        at, grad = self.at, self.grad
        self.aa.wait_recv()
        self.bb.wait_recv()

        def body(zz):
            grad[zz, at.y, at.x] = (
                grad[zz, at.y, at.x].astype(F32) + self.two[zz].astype(F32)
            ).astype(BF16)

        loop(NZ, body)
        self.z = [
            self.wire.copy(grad.at[at.ahead(step), at.y, at.x], self.three.at[step - 1], at.zn(step))
            for step in range(1, NZ)
        ]

    def result(self):
        at = self.at
        total = self.grad[at.z, at.y, at.x].astype(F32)
        for step in range(1, NZ):
            self.z[step - 1].wait_recv()
            total = total + self.three[step - 1].astype(F32)
        return total


def layer(unit, names, *refs):
    (
        seg_ref, freq_ref, mix_ref, gains_ref, in_ref, cot_ref,
        q_ref, k_ref, v_ref, o_ref, up_ref, down_ref, hist_ref,
        out_ref, gin_ref, gq_ref, gk_ref, gv_ref, go_ref, gup_ref, gdown_ref, small_ref,
    ) = refs[:22]
    s = dict(zip(names, refs[22:]))
    tokens, width = in_ref.shape
    length = 2 * tokens
    half = width // 2
    ff_half = up_ref.shape[1] // 2
    pairs = half // 128
    share = q_ref.shape[0]
    down_rows = down_ref.shape[0]
    blocks = length // BLOCK
    hist = hist_ref.shape[0]
    at = Place(unit)
    k, o = at.k, at.o
    wire = Wire(s["send"], s["recv"])

    hist_rows = s["hbuf"].shape[2]
    hist_chunks = tokens // hist_rows

    def fetch(i):
        return pltpu.make_async_copy(
            hist_ref.at[:, pl.ds(i * hist_rows, hist_rows)], s["hbuf"].at[i % 2], s["hsem"].at[i % 2]
        )

    fetch(0).start()

    xs, xr = s["xs"], s["xr"]
    qkv_cols = 3 * half
    blk = down_rows
    for h in range(2):
        c = h * half
        for i in range(pairs):
            for j, ref in enumerate((q_ref, k_ref, v_ref)):
                xs[h, :, 384 * i + 128 * j : 384 * i + 128 * j + 128] = ref[
                    :, c + 128 * i : c + 128 * i + 128
                ].astype(F32)
        xs[h, :, qkv_cols : qkv_cols + half] = o_ref[:, c : c + half].astype(F32)
        wide = up_ref[...].astype(F32)
        xs[h, :, qkv_cols + half :] = jnp.concatenate(
            [
                wide[:, 2 * blk * i + blk * h : 2 * blk * i + blk * h + blk]
                for i in range(GROUPS)
            ],
            axis=1,
        )
    ga = s["ga"]
    ga[k, at.z, at.y, at.x] = gains_ref[...]

    barrier = pltpu.get_barrier_semaphore()
    for device in (at.core, at.xn, at.yn, at.zn(1), at.zn(2), at.zn(3)):
        pl.semaphore_signal(barrier, inc=1, device_id=device, device_id_type=MESH)
    pl.semaphore_wait(barrier, 6)

    swap = wire.copy(xs.at[o], xr, at.core)
    gain_z = [
        wire.copy(ga.at[k, at.z, at.y, at.x], ga.at[k, at.z, at.y, at.x], at.zn(step))
        for step in range(1, NZ)
    ]
    s["wdown"][at.z, at.y, at.x] = down_ref[...]

    own0 = pl.multiple_of(k * tokens, tokens)
    other0 = pl.multiple_of(o * tokens, tokens)

    def own(i, size):
        return pl.ds(pl.multiple_of(own0 + i * size, size), size)

    def other(i, size):
        return pl.ds(pl.multiple_of(other0 + i * size, size), size)

    mix_last = mix_ref[hist]
    gbl, norm, sec, gfl = s["gbl"], s["norm"], s["sec"], s["gfl"]

    swap.wait_recv()
    mine = xs[k]
    theirs = xr[...]
    upper = jnp.where(k == 0, mine, theirs)
    lower = jnp.where(k == 0, theirs, mine)
    block = jnp.concatenate([upper, lower], axis=0).astype(BF16)
    s["wqkv"][at.z, at.y, at.x] = block[:, :qkv_cols]
    s["wo"][at.z, at.y, at.x] = block[:, qkv_cols : qkv_cols + half]
    s["wup"][at.z, at.y, at.x] = block[:, qkv_cols + half :]

    gather_qkv = Gather(wire, at, s["wqkv"], 640)
    gather_o = Gather(wire, at, s["wo"], 128)
    gather_up = Gather(wire, at, s["wup"], ff_half // 2)
    gather_down = Gather(wire, at, s["wdown"], half)
    gather_qkv.start()
    todo = gather_qkv.steps()[1:]

    def pump(count=1):
        for _ in range(count):
            if todo:
                todo.pop(0)()

    seg = seg_ref[...].astype(F32)
    seg_col = jnp.transpose(jnp.broadcast_to(seg, (128, length)))
    start_row = jnp.zeros((1, length), F32)
    start_col = jnp.zeros((length, 128), F32)
    for d in range(7):
        count = jnp.sum(jnp.where(seg == d, 1.0, 0.0), axis=1, keepdims=True)
        start_row = start_row + jnp.where(seg > d, count, 0.0)
        start_col = start_col + jnp.where(seg_col > d, count, 0.0)
    s["start_row"][...] = jnp.broadcast_to(start_row, (8, length))
    s["start_col"][...] = start_col
    lane = lax.broadcasted_iota(jnp.int32, (1, 128), 1)
    first_half = (lane % HD) < (HD // 2)

    for step in range(1, NZ):
        gain_z[step - 1].wait_recv()
    gain_x = wire.copy(ga.at[k, :, at.y, at.x], ga.at[k, :, at.y, at.x], at.xn)

    def rope_tables(i):
        rows = rows_of(i, 64)
        order = (lax.broadcasted_iota(jnp.int32, (64, 128), 0) + i * 64).astype(F32)
        angles = (order - s["start_col"][rows, :]) * freq_ref[0:1, :]
        s["cos"][rows, :] = jnp.cos(angles)
        sine = jnp.sin(angles)
        s["sin"][rows, :] = jnp.where(first_half, -sine, sine)

    loop(length // 64, rope_tables)
    gain_x.wait_recv()
    gain_y = wire.copy(ga.at[k, :, at.y], ga.at[k, :, at.y], at.yn)
    pump()

    def low_block(i):
        gbl[own(i, 32), :] = (mix_last * cot_ref[rows_of(i, 32), :].astype(F32)).astype(BF16)

    loop(tokens // 32, low_block)
    send_gbl = wire.copy(
        gbl.at[pl.ds(own0, tokens)], gbl.at[pl.ds(own0, tokens)], at.core
    )
    gain_y.wait_recv()
    gain_c = wire.copy(ga.at[k], ga.at[k], at.core)

    def history_chunk(i):
        if i + 1 < hist_chunks:
            fetch(i + 1).start()
        fetch(i).wait()

        def group(r, sums):
            rows = rows_of(r, 16)
            whole = pl.ds(pl.multiple_of(i * hist_rows + r * 16, 16), 16)
            cot = cot_ref[whole, :].astype(F32)
            total = jnp.zeros((16, width), F32)
            out = []
            for j in range(hist):
                earlier = s["hbuf"][i % 2, j, rows, :].astype(F32)
                total = total + mix_ref[j] * earlier
                term = fold_rows(earlier * cot)
                part = sums[j]
                for c in range(0, width, 128):
                    part = part + term[:, c : c + 128]
                out.append(part)
            s["acc"][whole, :] = total
            return tuple(out)

        sums = lax.fori_loop(
            0, hist_rows // 16, group, tuple(s["mixacc"][j] for j in range(hist))
        )
        for j in range(hist):
            s["mixacc"][j] = sums[j]

    s["mixacc"][...] = jnp.zeros_like(s["mixacc"])
    history_chunk(0)
    gain_c.wait_recv()

    lanes = lax.broadcasted_iota(jnp.int32, (128, width), 1).astype(F32)
    rows_i = lax.broadcasted_iota(jnp.int32, (128, width), 0)
    owner = jnp.floor((lanes + 0.5) * (1.0 / share))
    spread = jnp.where(lanes - share * owner == rows_i.astype(F32), 1.0, 0.0).astype(BF16)
    gain_rows = [jnp.zeros((1, width), F32), jnp.zeros((1, width), F32)]
    for kk in range(2):
        tiles = ga[kk].reshape(GROUPS * 8, 128).astype(BF16)
        wide = mm(tiles, spread)
        for r in range(2):
            hit = ((rows_i % 8) == r) & (owner == (2 * (rows_i // 8) + kk).astype(F32))
            gain_rows[r] = gain_rows[r] + jnp.sum(
                jnp.where(hit, wide, 0.0), axis=0, keepdims=True
            )
    s["gain"][...] = jnp.concatenate([gain_rows[0], gain_rows[1], jnp.zeros((6, width), F32)], axis=0)

    def norm_one(i):
        xhat, _ = normalize(in_ref[rows_of(i, 32), :].astype(F32))
        norm[own(i, 32), :] = (xhat * s["gain"][0:1, :]).astype(BF16)

    loop(tokens // 32, norm_one)
    send_norm = wire.copy(norm.at[pl.ds(own0, tokens)], norm.at[pl.ds(own0, tokens)], at.core)
    pump()
    for i in range(1, hist_chunks):
        history_chunk(i)
        if i % 2 == 0:
            pump()
    pump(4)
    gather_o.start()
    gather_up.start()
    todo.extend(gather_o.steps()[1:4])
    todo.append(lambda: (gather_o.pass_last(3), gather_up.pass_mid(1), gather_up.pass_last(0)))
    todo.append(gather_down.start)
    todo.extend(gather_up.steps()[2:])
    todo.extend(gather_down.steps()[1:])
    send_norm.wait_recv()
    send_gbl.wait_recv()
    gather_qkv.finish()

    qs, ks, vs = s["q"], s["kk"], s["v"]

    def turn(value, rows, sign):
        partner = jnp.where(first_half, pltpu.roll(value, 96, 1), pltpu.roll(value, 32, 1))
        return value * s["cos"][rows, :] + (sign * partner) * s["sin"][rows, :]

    def project(i):
        rows = rows_of(i, BLOCK)
        left = norm[rows, :]
        for p in range(pairs):
            wide = mm(left, s["wqkv"][:, :, :, :, 384 * p : 384 * p + 384].reshape(width, 384))
            cols = slice(128 * p, 128 * p + 128)
            qs[rows, cols] = (turn(wide[:, :128], rows, 1.0).astype(BF16) * HD**-0.5).astype(BF16)
            ks[rows, cols] = turn(wide[:, 128:256], rows, 1.0).astype(BF16)
            vs[rows, cols] = wide[:, 256:].astype(BF16)

    loop(blocks, project)
    pump()

    lane_low = lane < HD
    ones = [
        jnp.where(lane_low, 1.0, 0.0).astype(BF16),
        jnp.where(lane_low, 0.0, 1.0).astype(BF16),
    ]

    def attend(p, b):
        cols = slice(128 * p, 128 * p + 128)
        r0 = b * BLOCK
        rows = slice(r0, r0 + BLOCK)
        here_q = lax.broadcasted_iota(jnp.int32, (BLOCK, BLOCK), 0)
        here_k = lax.broadcasted_iota(jnp.int32, (BLOCK, BLOCK), 1)
        start = s["start_col"][rows, 0:1]
        outs, tops = [], []
        for h in range(2):
            query = qs[rows, cols] * ones[h]
            near = mm_nt(query, ks[rows, cols])
            near = jnp.where(
                (here_k <= here_q) & ((here_k + r0).astype(F32) >= start), near, MASKED
            )
            top = jnp.max(near, axis=1, keepdims=True)
            if b:
                far = mm_nt(query, ks[0:r0, cols])
                far_k = lax.broadcasted_iota(jnp.int32, (1, r0), 1).astype(F32)
                far = jnp.where(far_k >= start, far, MASKED)
                top = jnp.maximum(top, jnp.max(far, axis=1, keepdims=True))
            raw = jnp.exp(near - top).astype(BF16)
            out = mm(raw, vs[rows, cols] * ones[h] + ones[1 - h])
            if b:
                raw = jnp.exp(far - top).astype(BF16)
                out = out + mm(raw, vs[0:r0, cols] * ones[h] + ones[1 - h])
            outs.append(out)
            tops.append(top)
        total = jnp.where(lane_low, pltpu.roll(outs[0], HD, 1), pltpu.roll(outs[1], HD, 1))
        mixed = jnp.where(lane_low, outs[0], outs[1]) / total
        s["mix"][rows, cols] = mixed.astype(BF16)
        s["mixf"][rows, cols] = mixed
        log_total = jnp.transpose(jnp.where(lane_low, tops[0], tops[1]) + jnp.log(total))
        s["lse"][p, 0:1, rows] = log_total[0:1]
        s["lse"][p, 1:2, rows] = log_total[HD : HD + 1]

    for p in range(pairs):
        for b in range(blocks):
            attend(p, b)
            if b in (1, 3):
                pump()

    gather_o.finish()
    wo, wox = s["wo"], s["wox"]
    swap_o = wire.copy(wo.at[pl.ds(2 * o, 2)], wox, at.core)
    swap_o.wait_recv()
    my_cols = lane_cut(k * half, half)
    other_cols = lane_cut(o * half, half)

    def output_weight():
        return (
            wo[pl.ds(2 * k, 2)].reshape(half, half),
            wox[...].reshape(half, half),
        )

    part_s, part_r = s["part_s"], s["part_r"]
    quarter = tokens // 2

    def send_parts(make, store, recv):
        made = []
        for i in range(2):
            make(other(i, quarter), rows_of(i, quarter), store)
            made.append(
                wire.copy(
                    store.at[pl.ds(i * quarter, quarter)], recv.at[pl.ds(i * quarter, quarter)], at.core
                )
            )
        return made

    def attended(rows, to, store):
        left = s["mix"][rows, :]
        one, two = output_weight()
        store[to, my_cols] = mm(left, one)
        store[to, other_cols] = mm(left, two)

    arrive = send_parts(attended, part_s, part_r)
    first = s["first"]
    for i in range(2):
        attended(own(i, quarter), rows_of(i, quarter), first)
    pump()
    send_sec = []
    for i in range(2):
        arrive[i].wait_recv()

        def norm_two(j):
            rows = pl.ds(pl.multiple_of(i * quarter + j * 32, 32), 32)
            value = in_ref[rows, :].astype(F32) + (first[rows, :] + part_r[rows, :])
            first[rows, :] = value
            xhat, _ = normalize(value)
            to = pl.ds(pl.multiple_of(own0 + i * quarter + j * 32, 32), 32)
            sec[to, :] = (xhat * s["gain"][1:2, :]).astype(BF16)

        loop(quarter // 32, norm_two)
        send_sec.append(wire.copy(sec.at[own(i, quarter)], sec.at[own(i, quarter)], at.core))
    pump(9)
    gather_up.finish()
    hid, dgelu = s["hid"], s["dgelu"]
    wup, wdown = s["wup"], s["wdown"]
    sqrt_2_over_pi = float(np.sqrt(2.0 / np.pi).astype(np.float32))

    def expand(rows):
        left = sec[rows, :]
        step = 512
        for c in range(0, ff_half, step):
            v = mm(left, wup[:, :, :, :, c : c + step].reshape(width, step))
            vv = v * v
            t = jnp.tanh(sqrt_2_over_pi * (v + 0.044715 * (vv * v)))
            hid[rows, c : c + step] = (0.5 * v * (1.0 + t)).astype(BF16)
            dgelu[rows, c : c + step] = (
                0.5 * (1.0 + t)
                + (0.5 * sqrt_2_over_pi) * v * (1.0 - t * t) * (1.0 + 3 * 0.044715 * vv)
            ).astype(BF16)

    loop(tokens // 128, lambda j: expand(own(j, 128)))
    for i in range(2):
        send_sec[i].wait_recv()
        loop(quarter // 128, lambda j: expand(
            pl.ds(pl.multiple_of(other0 + i * quarter + j * 128, 128), 128)
        ))

    gdown = s["gdown"]

    def grad_down(zz):
        left = hid[:, pl.ds(pl.multiple_of(zz * 384, 128), 384)]
        wide = mm_tn(left, gbl[...]).astype(BF16)
        for i in range(2):
            gdown[i][zz] = wide[:, i * half : (i + 1) * half].reshape(NY, NX, down_rows, half)

    loop(NZ, grad_down)
    reduce_down = [
        Reduce(wire, at, gdown[i], (256, 128)[i], *s["rdown"][i]) for i in range(2)
    ]
    for r in reduce_down:
        r.first()
    pump(9)
    gather_down.finish()

    def back_hidden(rows, to, store):
        for j in range(rows.size // 128):
            part = pl.ds(pl.multiple_of(rows.start + j * 128, 128), 128)
            for c in range(0, ff_half, 512):
                weight = wdown[:, :, :, :, :].reshape(ff_half, width)[c : c + 512]
                grad = mm_nt(gbl[part, :], weight)
                dgelu[part, c : c + 512] = (
                    grad * dgelu[part, c : c + 512].astype(F32)
                ).astype(BF16)
        store[to, :] = mm_nt(dgelu[rows, :], wup[...].reshape(width, ff_half))

    for made in arrive:
        wire.sent(made)
    arrive = send_parts(back_hidden, part_s, part_r)
    gsec = s["gfirst"]
    for i in range(2):
        back_hidden(own(i, quarter), rows_of(i, quarter), gsec)
    gup = s["gup"]

    def grad_up(j):
        left = sec[:, pl.ds(pl.multiple_of(j * 384, 128), 384)]
        for i in range(2):
            wide = mm_tn(left, dgelu[:, i * width : (i + 1) * width]).astype(BF16)
            gup[i][pl.ds(2 * j, 2)] = wide.reshape(2, NY, NX, 2 * share, width)

    small = s["small"]
    small[...] = jnp.zeros_like(small)

    def norm_two_back(i):
        arrive[i].wait_recv()

        def body(j, total):
            rows = pl.ds(pl.multiple_of(i * quarter + j * 32, 32), 32)
            grad = gsec[rows, :] + part_r[rows, :]
            xhat, root = normalize(first[rows, :])
            part = norm_back(xhat, root, s["gain"][1:2, :], grad)
            full = mix_last * cot_ref[rows, :].astype(F32) + part
            gsec[rows, :] = full
            to = pl.ds(pl.multiple_of(own0 + i * quarter + j * 32, 32), 32)
            gfl[to, :] = full.astype(BF16)
            return total + fold_rows(grad * xhat)

        total = lax.fori_loop(0, quarter // 32, body, jnp.zeros((8, width), F32))
        small[1:2, :] = small[1:2, :] + jnp.sum(total, axis=0, keepdims=True)
        return wire.copy(gfl.at[own(i, quarter)], gfl.at[own(i, quarter)], at.core)

    send_gfl = [norm_two_back(0), norm_two_back(1)]
    loop(2, grad_up)
    reduce_up = [
        Reduce(wire, at, gup[i], width // 2, *s["rup"][i]) for i in range(2)
    ]
    for r in reduce_up:
        r.first()
    for r in reduce_down:
        r.second()

    out_s, out_r = s["out_s"], s["out_r"]

    def contract(rows, to, store):
        store[to, :] = mm(hid[rows, :], wdown[...].reshape(ff_half, width))

    arrive_out = send_parts(contract, out_s, out_r)

    gm = s["gm"]

    def back_mixed(rows):
        one, two = output_weight()
        left = gfl[rows, my_cols]
        right = gfl[rows, other_cols]
        gm[rows, :] = (mm_nt(left, one) + mm_nt(right, two)).astype(BF16)

    back_mixed(own(0, tokens))
    for made in send_gfl:
        made.wait_recv()
    back_mixed(other(0, tokens))
    go = s["go"]
    left = s["mix"][...]
    go[pl.ds(2 * k, 2)] = mm_tn(left, gfl[:, my_cols]).astype(BF16).reshape(
        2, NY, NX, 2 * share, half
    )
    s["gox"][...] = mm_tn(left, gfl[:, other_cols]).astype(BF16).reshape(
        2, NY, NX, 2 * share, half
    )
    swap_go = wire.copy(s["gox"], go.at[pl.ds(2 * k, 2)], at.core)

    outb = s["outb"]
    block_sum = jnp.zeros((8, width), F32)
    for i in range(2):
        rows = pl.ds(i * quarter, quarter)
        mine_out = out_s
        wire.sent(arrive_out[i])
        contract(own(i, quarter), rows, mine_out)
        arrive_out[i].wait_recv()

        def finish_out(j, total):
            part = pl.ds(pl.multiple_of(i * quarter + j * 32, 32), 32)
            block = first[part, :] + (mine_out[part, :] + out_r[part, :])
            outb[part, :] = (s["acc"][part, :] + mix_last * block).astype(BF16)
            return total + fold_rows(block * cot_ref[part, :].astype(F32))

        block_sum = lax.fori_loop(0, quarter // 32, finish_out, block_sum)
    put_out = pltpu.make_async_copy(outb, out_ref, s["osem"].at[0])
    put_out.start()
    terms = jnp.zeros((1, width), F32)
    wide_lane = lax.broadcasted_iota(jnp.int32, (1, width), 1)
    for j in range(hist):
        terms = jnp.where(wide_lane == j, jnp.sum(s["mixacc"][j]), terms)
    terms = jnp.where(wide_lane == hist, jnp.sum(block_sum), terms)
    small[2:3, :] = terms
    swap_go.wait_recv()
    reduce_o = Reduce(wire, at, go, 128, *s["ro"])
    reduce_o.first()

    todo.extend([r.second for r in reduce_up])
    todo.extend([r.third for r in reduce_down])
    todo.append(reduce_o.second)
    todo.extend([r.third for r in reduce_up])
    todo.append(reduce_o.third)

    lse, delta = s["lse"], s["delta"]
    gqkv = s["hid"]
    gpair = s["gqkv"]
    grad_query = s["dq"]
    reduce_qkv = [
        Reduce(wire, at, gpair[p], (256, 128, 256)[p % 3], *s["rqkv"][p]) for p in range(pairs)
    ]

    def attend_back(p, b):
        cols = slice(128 * p, 128 * p + 128)
        r0 = b * BLOCK
        rows = slice(r0, r0 + BLOCK)
        after = slice(r0, length)
        count = length - r0
        here_k = lax.broadcasted_iota(jnp.int32, (BLOCK, count), 0)
        here_q = lax.broadcasted_iota(jnp.int32, (BLOCK, count), 1)
        allowed = (here_k <= here_q) & (
            (here_k + r0).astype(F32) >= s["start_row"][0:1, after]
        )
        key, value = ks[rows, cols], vs[rows, cols]
        query, grad = qs[after, cols], gm[after, cols]
        dk = jnp.zeros((BLOCK, 128), F32)
        dv = jnp.zeros((BLOCK, 128), F32)
        dq = jnp.zeros((count, 128), F32)
        for h in range(2):
            key_h = key * ones[h]
            scores = mm_nt(key_h, query)
            weights = jnp.exp(jnp.where(allowed, scores - lse[p, h : h + 1, after], MASKED))
            grad_w = mm_nt(value * ones[h], grad)
            grad_s = (weights * (grad_w - delta[p, h : h + 1, after])).astype(BF16)
            dv = dv + mm(weights.astype(BF16), grad * ones[h])
            dk = dk + mm(grad_s, query * ones[h])
            dq = dq + mm_tn(grad_s, key_h)
        base = 384 * p
        gqkv[rows, base + 256 : base + 384] = dv.astype(BF16)
        gqkv[rows, base + 128 : base + 256] = turn(
            dk.astype(BF16).astype(F32), rows, -1.0
        ).astype(BF16)
        if b == 0:
            grad_query[...] = dq
        else:
            grad_query[after, :] = grad_query[after, :] + dq

    for p in range(pairs):
        cols = slice(128 * p, 128 * p + 128)

        def inner(i):
            rows = rows_of(i, BLOCK)
            both = jnp.transpose(s["mixf"][rows, cols] * gm[rows, cols].astype(F32))
            delta[p, 0:1, rows] = jnp.sum(both[:HD], axis=0, keepdims=True)
            delta[p, 1:2, rows] = jnp.sum(both[HD:], axis=0, keepdims=True)

        loop(blocks, inner)
        for b in range(blocks):
            attend_back(p, b)
            if b in (1, 3):
                pump()

        def turn_query(i):
            rows = rows_of(i, BLOCK)
            low = (grad_query[rows, :] * HD**-0.5).astype(BF16).astype(F32)
            gqkv[rows, 384 * p : 384 * p + 128] = turn(low, rows, -1.0).astype(BF16)

        loop(blocks, turn_query)

        def grad_qkv(j):
            left = norm[:, pl.ds(pl.multiple_of(j * 384, 128), 384)]
            wide = mm_tn(left, gqkv[:, 384 * p : 384 * p + 384]).astype(BF16)
            gpair[p][pl.ds(2 * j, 2)] = wide.reshape(2, NY, NX, 2 * share, 384)

        loop(2, grad_qkv)
        reduce_qkv[p].first()
        if p:
            reduce_qkv[p - 1].second()
        if p > 1:
            reduce_qkv[p - 2].third()

    for made in arrive:
        wire.sent(made)

    def back_normed(rows, to, store):
        store[to, :] = mm_nt(gqkv[rows, :qkv_cols], s["wqkv"][...].reshape(width, qkv_cols))

    arrive = send_parts(back_normed, part_s, part_r)
    reduce_qkv[pairs - 1].second()
    pump(9)
    if pairs > 1:
        reduce_qkv[pairs - 2].third()
    own_s = out_s
    for i in range(2):
        back_normed(own(i, quarter), rows_of(i, quarter), own_s)
    reduce_qkv[pairs - 1].third()
    total = jnp.zeros((8, width), F32)
    for i in range(2):
        arrive[i].wait_recv()

        def norm_one_back(j, total):
            rows = pl.ds(pl.multiple_of(i * quarter + j * 32, 32), 32)
            grad = own_s[rows, :] + part_r[rows, :]
            xhat, root = normalize(in_ref[rows, :].astype(F32))
            gsec[rows, :] = gsec[rows, :] + norm_back(xhat, root, s["gain"][0:1, :], grad)
            return total + fold_rows(grad * xhat)

        total = lax.fori_loop(0, quarter // 32, norm_one_back, total)
    put_gin = pltpu.make_async_copy(gsec, gin_ref, s["osem"].at[1])
    put_gin.start()
    small[0:1, :] = jnp.sum(total, axis=0, keepdims=True)

    sr, sz = s["small_r"], s["small_z"]
    step_c = wire.copy(small, sr.at[0], at.core)

    fin, fin_r = s["fin"], s["fin_r"]
    mine_rows = pl.ds(pl.multiple_of(k * share, 8), share)
    other_rows = pl.ds(pl.multiple_of(o * share, 8), share)

    def settle(reduce, c, size):
        fin[:, c : c + size] = reduce.result()
        return wire.copy(
            fin.at[other_rows, pl.ds(c, size)], fin_r.at[:, pl.ds(c, size)], at.core
        )

    for i in range(2):
        gdown_ref[:, i * half : (i + 1) * half] = reduce_down[i].result()
    up0 = qkv_cols + half
    settled = [settle(reduce_up[i], up0 + i * width, width) for i in range(2)]
    settled.append(settle(reduce_o, qkv_cols, half))
    step_c.wait_recv()
    s["small1"][...] = small[...] + sr[0]
    step_y = wire.copy(s["small1"], sr.at[1], at.yn)
    for p in range(pairs - 1):
        settled.append(settle(reduce_qkv[p], 384 * p, 384))
    step_y.wait_recv()
    s["small2"][...] = s["small1"][...] + sr[1]
    step_x = wire.copy(s["small2"], sr.at[2], at.xn)
    settled.append(settle(reduce_qkv[pairs - 1], 384 * (pairs - 1), 384))
    step_x.wait_recv()
    sz[at.z] = s["small2"][...] + sr[2]
    step_z = [wire.copy(sz.at[at.z], sz.at[at.z], at.zn(step)) for step in range(1, NZ)]
    for made in settled:
        made.wait_recv()
    for p in range(pairs):
        for j, ref in enumerate((gq_ref, gk_ref, gv_ref)):
            c = 384 * p + 128 * j
            ref[:, lane_cut(k * half + 128 * p, 128)] = fin[mine_rows, c : c + 128]
            ref[:, lane_cut(o * half + 128 * p, 128)] = fin_r[:, c : c + 128]
    go_ref[:, my_cols] = fin[mine_rows, qkv_cols:up0]
    go_ref[:, other_cols] = fin_r[:, qkv_cols:up0]
    gup_ref[k] = fin[mine_rows, up0:]
    gup_ref[o] = fin_r[:, up0:]
    for made in step_z:
        made.wait_recv()
    small_ref[...] = ((sz[0] + sz[1]) + sz[2]) + sz[3]
    put_out.wait()
    put_gin.wait()
    wire.close()


def local(
    unit,
    devices,
    inputs,
    history,
    segment_ids,
    cotangent,
    mix_weights,
    attn_gain,
    query_weight,
    key_weight,
    value_weight,
    output_weight,
    mlp_gain,
    up_weight,
    down_weight,
):
    rows, tokens, width = inputs.shape
    hist = history.shape[0]
    length = segment_ids.shape[1]
    half = width // 2
    ff_half = up_weight.shape[1] // 2
    share = width // (2 * GROUPS)
    both = 2 * share
    down_share = 2 * ff_half // (2 * GROUPS)
    pairs = half // 128
    seq = lax.axis_index("seq")
    batch = lax.axis_index("batch")
    group_device = (batch // unit) * 2 + seq
    weights = [query_weight, key_weight, value_weight, output_weight, up_weight, down_weight]
    gains = [attn_gain, mlp_gain]
    if unit > 1:
        def widen(value):
            whole = lax.all_gather(value, ("batch", "seq"), axis=0, tiled=True)
            size = value.shape[0] * unit
            return lax.dynamic_slice_in_dim(whole, group_device * size, size)

        weights = [widen(value) for value in weights]
        gains = [widen(value) for value in gains]
    gain_tile = jnp.pad(jnp.stack(gains).astype(F32), ((0, 6), (0, 128 - share)))
    freq = (10000.0 ** (-(2.0 / HD) * (np.arange(128) % (HD // 2)))).astype(np.float32)
    freq = jnp.asarray(np.broadcast_to(freq, (8, 128)))

    sizes = []

    def scratch(name, shape, dtype=BF16):
        sizes.append((name, pltpu.VMEM(shape, dtype)))

    dims = (NZ, NY, NX)

    def reduction(rows_in, columns, cut):
        return [
            pltpu.VMEM((NZ, NX, rows_in, cut), BF16),
            pltpu.VMEM((NZ, NY, rows_in, columns - cut), BF16),
            pltpu.VMEM((NZ, rows_in, columns), BF16),
            pltpu.VMEM((NZ - 1, rows_in, columns), BF16),
        ]

    sizes.append(("send", pltpu.SemaphoreType.DMA((COPIES,))))
    sizes.append(("recv", pltpu.SemaphoreType.DMA((COPIES,))))
    sizes.append(("hsem", pltpu.SemaphoreType.DMA((2,))))
    sizes.append(("osem", pltpu.SemaphoreType.DMA((2,))))
    scratch("hbuf", (2, hist, 32, width))
    scratch("xs", (2, share, 2 * half + 2 * half + ff_half), F32)
    scratch("xr", (share, 2 * half + 2 * half + ff_half), F32)
    scratch("ga", (2,) + dims + (8, 128), F32)
    scratch("gain", (8, width), F32)
    scratch("wqkv", dims + (both, 3 * half))
    scratch("wo", dims + (both, half))
    scratch("wox", (2, NY, NX, both, half))
    scratch("wup", dims + (both, ff_half))
    scratch("wdown", dims + (down_share, width))
    for name in ("gbl", "norm", "sec", "gfl"):
        scratch(name, (length, width))
    scratch("start_row", (8, length), F32)
    scratch("start_col", (length, 128), F32)
    scratch("cos", (length, 128), F32)
    scratch("sin", (length, 128), F32)
    scratch("acc", (tokens, width), F32)
    scratch("mixacc", (hist, 8, 128), F32)
    for name in ("q", "kk", "v", "mix", "gm"):
        scratch(name, (length, half))
    scratch("mixf", (length, half), F32)
    scratch("lse", (pairs, 8, length), F32)
    scratch("delta", (pairs, 8, length), F32)
    scratch("dq", (length, 128), F32)
    for name in ("part_s", "part_r", "out_s", "out_r", "first", "gfirst"):
        scratch(name, (tokens, width), F32)
    scratch("outb", (tokens, width))
    scratch("hid", (length, ff_half))
    scratch("dgelu", (length, ff_half))
    scratch("gox", (2, NY, NX, both, half))
    for name in ("small", "small1", "small2"):
        scratch(name, (8, width), F32)
    scratch("small_r", (3, 8, width), F32)
    scratch("small_z", (NZ, 8, width), F32)
    scratch("fin", (both, 4 * half + ff_half), F32)
    scratch("fin_r", (share, 4 * half + ff_half), F32)
    sizes.append(("gdown", [pltpu.VMEM(dims + (down_share, half), BF16) for _ in range(2)]))
    sizes.append(("gup", [pltpu.VMEM(dims + (both, width), BF16) for _ in range(2)]))
    scratch("go", dims + (both, half))
    sizes.append(("gqkv", [pltpu.VMEM(dims + (both, 384), BF16) for _ in range(pairs)]))
    sizes.append(("rdown", [reduction(down_share, half, cut) for cut in (256, 128)]))
    sizes.append(("rup", [reduction(both, width, width // 2) for _ in range(2)]))
    sizes.append(("ro", reduction(both, half, 128)))
    sizes.append(("rqkv", [reduction(both, 384, (256, 128, 256)[p % 3]) for p in range(pairs)]))
    names = [name for name, _ in sizes]

    vmem = pl.BlockSpec(memory_space=pltpu.VMEM)
    anywhere = pl.BlockSpec(memory_space=pl.ANY)
    smem = pl.BlockSpec(memory_space=pltpu.SMEM)
    shape = jax.ShapeDtypeStruct
    outs = pl.pallas_call(
        functools.partial(layer, unit, names),
        out_shape=(
            shape((tokens, width), BF16),
            shape((tokens, width), F32),
            shape((share, width), F32),
            shape((share, width), F32),
            shape((share, width), F32),
            shape((share, width), F32),
            shape((2, share, ff_half), F32),
            shape((down_share, width), F32),
            shape((8, width), F32),
        ),
        in_specs=[vmem, vmem, smem] + [vmem] * 9 + [anywhere],
        out_specs=[anywhere, anywhere] + [vmem] * 7,
        scratch_shapes=[size for _, size in sizes],
        compiler_params=pltpu.CompilerParams(
            collective_id=0, has_side_effects=True, vmem_limit_bytes=64 * 1024 * 1024 - 64 * 1024
        ),
    )(
        segment_ids,
        freq,
        mix_weights,
        gain_tile,
        inputs.reshape(tokens, width),
        cotangent.reshape(tokens, width),
        *weights,
        history.reshape(hist, tokens, width),
    )
    output, grad_inputs, gq, gk, gv, go, gup, gdown, small = outs
    gup = (
        gup.reshape(2, share, GROUPS, down_share)
        .transpose(1, 2, 0, 3)
        .reshape(share, 2 * ff_half)
    )
    grads = [gq, gk, gv, go, gup, gdown]
    mix_grad = small[2, : hist + 1]
    device = batch * 2 + seq
    size = width // devices
    if unit > 1:
        def narrow(value):
            whole = jnp.zeros((value.shape[0] * 2 * GROUPS,) + value.shape[1:], F32)
            whole = lax.dynamic_update_slice_in_dim(whole, value, group_device * value.shape[0], 0)
            return lax.psum_scatter(whole, ("batch", "seq"), scatter_dimension=0, tiled=True)

        grads = [narrow(value) for value in grads]
        small = lax.psum(small, ("batch", "seq")) / (2 * GROUPS)
        mix_grad = small[2, : hist + 1]
    gain_one = lax.dynamic_slice(small, (0, device * size), (1, size))[0]
    gain_two = lax.dynamic_slice(small, (1, device * size), (1, size))[0]
    grad_history = (
        mix_weights[:-1, None, None, None] * cotangent.astype(F32)[None]
    ).astype(BF16)
    return (
        output.reshape(rows, tokens, width),
        grad_inputs.reshape(rows, tokens, width),
        grad_history,
        mix_grad,
        gain_one,
        grads[0],
        grads[1],
        grads[2],
        grads[3],
        gain_two,
        grads[4],
        grads[5],
    )


def solution(mesh):
    batch = mesh.shape["batch"]
    split = P(("batch", "seq"), None)
    gain = P(("batch", "seq"))
    placed = (
        P("batch", "seq", None),
        P(None, "batch", "seq", None),
        P("batch", None),
        P("batch", "seq", None),
        P(),
        gain,
        split,
        split,
        split,
        split,
        gain,
        split,
        split,
    )
    return jax.shard_map(
        functools.partial(local, batch // GROUPS, 2 * batch),
        mesh=mesh,
        in_specs=placed,
        out_specs=(
            P("batch", "seq", None),
            P("batch", "seq", None),
            P(None, "batch", "seq", None),
            P(),
            gain,
            split,
            split,
            split,
            split,
            gain,
            split,
            split,
        ),
        check_vma=False,
    )
```

time: 1140 us -> 209 us (0.18)
  waiting for transfers between devices: 600 us -> 0 us
  Pallas kernels: 0 us -> 181 us
  matrix products: 136 us -> 0 us
  blocking collectives: 130 us -> 0 us
  local copies, waits for them, and re-layouts: 125 us -> 11.9 us
  other arithmetic: 119 us -> 11.1 us
  between operations: 15.3 us -> 0.96 us
    reduce_scatter x6 -> x0, waiting for transfers between devices: 438 us -> none  [the longest x1 142 us: local(): lax.psum_scatter(grad_up, ('batch', 'seq'), scatter_dimension=0, tiled=True)]
    pallas_call x0 -> x1, Pallas kernels: none -> 181 us  [local(): pl.pallas_call(functools.partial(layer, unit, names), out_shape=(shape((t...]
    all_gather x6 -> x0, waiting for transfers between devices: 158 us -> none  [the longest x1 57 us: local(): lax.all_gather(down_weight, ('batch', 'seq'), axis=0, tiled=True)]
    dot_general x30 -> x0, matrix products: 136 us -> none  [the longest x6 28.3 us: contract_rows(): lax.dot_general(left, right, (((0,), (0,)), ((), ())), preferred_element_...]
    unnamed x11 -> x0, other arithmetic: 57.9 us -> none
    unnamed x121 -> x21, local copies, waits for them, and re-layouts: 61.9 us -> 5.3 us
    all_to_all x8 -> x0, blocking collectives: 47.8 us -> none  [the longest x1 6.75 us: local(): lax.all_to_all(for_sending(mixed_heads), 'seq', split_axis=1, concat_axis...]
    unnamed x1 -> x0, blocking collectives: 42 us -> none
  transfers between devices with their start and end apart: 12 -> 0, of which waited for: 9 -> 0; matrix products, arithmetic and copies ran while one was open for 28% -> 0% of each run, Pallas kernels for 0% -> 0%
where the time goes in v1:
time: 209 us; the launch traced here: 205 us
  Pallas kernels  181 us (87%)
  local copies, waits for them, and re-layouts  11.9 us (6%)
  other arithmetic  11.1 us (5%)
    pallas_call x1, Pallas kernels, local(): pl.pallas_call(functools.partial(layer, unit, names), out_shape=(shape((t...  181 us
    convert_element_type x1, other arithmetic, local(): grad_history = (mix_weights[:-1, None, None, None] * cotangent.astype(F32...  7.47 us
    unnamed x21, local copies, waits for them, and re-layouts  5.3 us

profile of v1, /device:TPU:0, one launch (start us, length us, event | category | flops | bytes accessed | tf_op | source)
XLA Modules:
  0.0 205.4 jit_solution(12818009327015370595)
XLA Ops:
  0.7 1.3 fusion.6.refs_3_
  1.9 2.4 %bitcast_convert_fusion = f32[512,768]{1,0:T(8,128)} fusion(bf16[1,512,768]{2,1,0:T(8,128)(2,1)} %param.17), kind=kLoop, calls=%fused_computation.13 | loop fusion | flops 393216 | bytes 2359296 | tf_op jit(solution)/shard_map/mul | solution.py:1058
  4.3 1.2 jit_solution_.3.refs_1_
  5.6 181.4 %shard_map.229 = (bf16[512,768]{1,0:T(8,128)(2,1)}, f32[512,768]{1,0:T(8,128)}, f32[24,768]{1,0:T(8,128)}, f32[24,768]{1,0:T(8,128)}, f32[24,768]{1,0:T(8,128)},...) custom-call(s32[1,1024]{1,0:T(1,128)} %refs_0_.1, ...), custom_call_target="tpu_custom_call" | custom-call | tf_op jit(solution)/shard_map/pallas_call | solution.py:1007
  187.0 0.0 copy-start.1
  187.0 0.0 copy-start
  187.0 0.0 copy-start.3
  187.0 0.0 copy-start.2
  187.0 1.3 slice_bitcast_fusion
  188.4 1.4 dynamic-slice_bitcast_fusion
  189.7 1.1 reshape.65
  190.8 0.3 copy.26
  191.2 0.0 copy-start.6
  191.2 0.0 copy-start.5
  191.2 0.0 copy-start.4
  191.2 1.2 reshape.66
  192.4 7.5 %multiply_convert_fusion = bf16[12,1,512,768]{3,2,1,0:T(8,128)(2,1)} fusion(f32[512,768]{1,0:T(8,128)} %bitcast_convert_fusion, f32[12]{0:T(128)} %bitcast.22), kind=kLoop, calls=%fused_computation | loop fusion | flops 9437184 | bytes 11010096 | tf_op jit(solution)/shard_map/convert_element_type | solution.py:1059
  199.9 0.0 copy-done.1
  199.9 0.9 copy.34
  200.8 0.0 copy-done
  200.8 1.1 copy.35
  201.9 0.0 copy-done.6
  201.9 0.6 copy.36
  202.6 0.0 copy-done.5
  202.6 0.6 copy.37
  203.2 0.0 copy-done.4
  203.2 0.6 copy.38
  203.8 0.0 copy-done.3
  203.8 0.6 copy.39
  204.5 0.0 copy-done.2
  204.5 0.7 copy.40
Async XLA Ops:
  187.0 12.9 %copy-start.1 = (bf16[512,768]{1,0:T(8,128)(2,1)S(1)}, bf16[512,768]{1,0:T(8,128)(2,1)}, u32[]{:S(2)}) copy-start(bf16[512,768]{1,0:T(8,128)(2,1)} %get-tuple-element.21) | copy-start | bytes 2359300
  187.0 13.8 %copy-start = (f32[512,768]{1,0:T(8,128)S(1)}, f32[512,768]{1,0:T(8,128)}, u32[]{:S(2)}) copy-start(f32[512,768]{1,0:T(8,128)} %get-tuple-element.22) | copy-start | bytes 4718596
  187.0 16.8 %copy-start.3 = (f32[24,768]{1,0:T(8,128)S(1)}, f32[24,768]{1,0:T(8,128)}, u32[]{:S(2)}) copy-start(f32[24,768]{1,0:T(8,128)} %get-tuple-element.52) | copy-start | bytes 221188
  187.0 17.4 %copy-start.2 = (f32[96,768]{1,0:T(8,128)S(1)}, f32[96,768]{1,0:T(8,128)}, u32[]{:S(2)}) copy-start(f32[96,768]{1,0:T(8,128)} %get-tuple-element.55) | copy-start | bytes 884740
  191.2 10.8 %copy-start.6 = (f32[24,768]{1,0:T(8,128)S(1)}, f32[24,768]{1,0:T(8,128)}, u32[]{:S(2)}) copy-start(f32[24,768]{1,0:T(8,128)} %get-tuple-element.49) | copy-start | bytes 221188
  191.2 11.4 %copy-start.5 = (f32[24,768]{1,0:T(8,128)S(1)}, f32[24,768]{1,0:T(8,128)}, u32[]{:S(2)}) copy-start(f32[24,768]{1,0:T(8,128)} %get-tuple-element.50) | copy-start | bytes 221188
  191.2 12.0 %copy-start.4 = (f32[24,768]{1,0:T(8,128)S(1)}, f32[24,768]{1,0:T(8,128)}, u32[]{:S(2)}) copy-start(f32[24,768]{1,0:T(8,128)} %get-tuple-element.51) | copy-start | bytes 221188
